TPU v7x, 128 devices: a whole 4x4x4 slice. The times are simulated.
128 devices in a mesh: cells: 16 (over z, x), sub: 8 (over y, core).
Axes of the slice: x: 4, y: 4, z: 4, core: 2. Of those that a mesh axis runs over, the one named last changes fastest.
Arguments:
- send_cells: int32 [128, 128, 1], P(('cells', 'sub')), may hold values from -1 to 15, as said below
- pair_cell: int32 [128, 128, 1], P(('cells', 'sub')), may hold values from 0 to 15
- counts: int32 [2048], P(('cells', 'sub')), may hold values from 1 to 128, as said below
- positions: float32 [3, 2048, 128], P(None, ('cells', 'sub')), may hold values from 0 to 1.5, as said below
- mass: float32 [2048, 128], P(('cells', 'sub')), may hold values from 0.004 to 0.016
- smooth: float32 [2048, 128], P(('cells', 'sub')), may hold values from 0.5 to 1
- entropy: float32 [2048, 128], P(('cells', 'sub')), may hold values from 0.5 to 2
Outputs:
- density: float32 [2048, 128], P(('cells', 'sub'))
- accel: float32 [3, 2048, 128], P(None, ('cells', 'sub'))
Inputs may be any that keep to these rules, and one draw needn't show every extreme that they name: send_cells[p, q, k] is the index within device p of a cell that p pairs with device q, or -1 for an empty slot; the cells that p names for one q are distinct; send_cells[p, p, k] = -1. `counts`: slots of a cell at or above its count are padding; whole devices differ in their cells' occupancy. `positions`: each cell's particles lie in a unit cube of its own, whose corner lies in [0, 0.5] along each component.
All inputs are finite; a program needn't handle non-finite values.
Results may differ from a plain program's by a relative error of at most 0.00016.
Values sent between devices are 32-bit elements; how exact they have to be, the bound alone decides.
A program may use at most 64 MiB of HBM per device.

v0:
```python
import functools
import math

import jax
import jax.numpy as jnp
from jax import lax
from jax.experimental import pallas as pl
from jax.experimental.pallas import tpu as pltpu
from jax.sharding import PartitionSpec as P

KERNEL_NORM = 21.0 / (2.0 * math.pi)
CENTRE = 0.75
CHUNK = 64
LOGICAL = pl.DeviceIdType.LOGICAL
F32 = jnp.float32
BF16 = jnp.bfloat16


def rounded(value):
    return value.astype(BF16).astype(F32)


def three_pieces(value):
    first = rounded(value)
    rest = value - first
    second = rounded(rest)
    return first, second, rest - second


def dot_rows(left, right):
    return lax.dot_general(left, right, (((1,), (1,)), ((), ())), preferred_element_type=F32)


def dot_plain(left, right):
    return lax.dot_general(left, right, (((1,), (0,)), ((), ())), preferred_element_type=F32)


def pair_kernel(
    ring,
    peers,
    cells,
    slots,
    send_s,
    pair_s,
    counts_s,
    send_ref,
    pair_ref,
    pos_ref,
    mass_ref,
    smooth_ref,
    entropy_ref,
    out_ref,
    table,
    table_len,
    table_press,
    table_gap,
    columns,
    fourths,
    aug,
    out_msg,
    in_msg,
    out_press,
    in_press,
    source_rows,
    source_stack,
    dist,
    near_mats,
    far_mats,
    results,
    send_sem,
    recv_sem,
    send_sem2,
    recv_sem2,
    ready_sem,
):
    me = lax.axis_index(("cells", "sub"))
    local_next = cells - 1
    local_own = cells // 2
    local_count = local_next + local_own
    total_count = local_count + peers - 1
    stride = results.shape[0] // 8

    barrier = pltpu.get_barrier_semaphore()
    for step in range(1, ring):
        pl.semaphore_signal(barrier, inc=1, device_id=me ^ step, device_id_type=LOGICAL)
    for step in range(1, peers // ring):
        pl.semaphore_signal(
            barrier, inc=1, device_id=me ^ (ring * step), device_id_type=LOGICAL
        )

    row = lax.broadcasted_iota(jnp.int32, (8, slots), 0)
    upper = row < 4
    weight_row = (row == 3) | (row == 7)
    lane = lax.broadcasted_iota(jnp.int32, (1, slots), 1)

    for cell in range(cells):
        mass_row = jnp.where(lane < counts_s[cell], mass_ref[cell : cell + 1, :], 0.0)
        for half in (0, 4):
            for axis in range(3):
                row_at = half + axis
                table[cell, row_at : row_at + 1, :] = pos_ref[axis, cell : cell + 1, :] - CENTRE
            table[cell, half + 3 : half + 4, :] = mass_row
    table[cells] = jnp.zeros((8, slots), F32)
    for cell in range(cells):
        table_len[cell] = jnp.broadcast_to(smooth_ref[cell : cell + 1, :], (8, slots))
    table_len[cells] = jnp.ones((8, slots), F32)
    table_press[cells] = jnp.zeros((8, slots), F32)
    results[...] = jnp.zeros(results.shape, F32)

    def fill_out(step, carry):
        peer = me ^ step
        chosen = send_s[0, peer]
        first = jnp.where(chosen < 0, cells, chosen)
        second = pair_s[0, peer]
        out_msg[step, 0:8, :] = jnp.where(upper, table[first], table[second])
        out_msg[step, 8:10, :] = jnp.where(row < 1, table_len[first], table_len[second])[0:2, :]
        return carry

    lax.fori_loop(0, peers, fill_out, 0, unroll=4)

    def fill_local(index, first, second):
        in_msg[peers + index, 0:8, :] = jnp.where(upper, table[first], table[second])
        in_msg[peers + index, 8:9, :] = table_len[first, 0:1, :]
        in_msg[peers + index, 9:10, :] = table_len[second, 0:1, :]

    for cell in range(local_next):
        fill_local(cell, cell + 1, cell)
    for turn in range(local_own):
        fill_local(local_next + turn, 2 * turn, 2 * turn + 1)

    blank = jnp.zeros((8, slots), F32)
    for cell in range(cells):
        own = table[cell]
        square = own * own
        total = pltpu.roll(square, 1, 0) + pltpu.roll(square, 2, 0) + pltpu.roll(square, 3, 0)
        own_len = table_len[cell]
        table_gap[cell] = own_len * own_len - total
        p0, p1, p2 = three_pieces(jnp.where(weight_row, total, own))
        one = jnp.ones((8, slots), F32)
        q0 = jnp.where(weight_row, one, -2.0 * p0)
        q1 = jnp.where(weight_row, p0, -2.0 * p1)
        q2 = jnp.where(weight_row, p1, -2.0 * p2)
        q4 = jnp.where(weight_row, p2, -2.0 * p1)
        parts = [jnp.where(upper, q0, q1), jnp.where(upper, q2, q0), jnp.where(upper, q4, q0)]
        aug[cell, 0] = jnp.concatenate(parts + [blank] * 5, axis=0).astype(BF16)
        aug[cell, 1] = jnp.concatenate([blank] * 3 + parts + [blank] * 2, axis=0).astype(BF16)

    pl.semaphore_wait(barrier, ring + peers // ring - 2)
    for step in range(1, ring):
        pl.semaphore_signal(ready_sem, inc=1, device_id=me ^ step, device_id_type=LOGICAL)

    def copy_out(step, source, target, sent, received):
        pltpu.make_async_remote_copy(
            src_ref=source.at[step],
            dst_ref=target.at[step],
            send_sem=sent,
            recv_sem=received.at[(step + 2) // 4],
            device_id=me ^ step,
            device_id_type=LOGICAL,
        ).start()

    def wait_in(group, count, ref, sem):
        got = ref.at[pl.ds(0, count)]
        pltpu.make_async_copy(got, got, sem.at[group]).wait()

    def slot_of(turn):
        return jnp.where(turn < local_count, peers + turn, turn - local_count + 1)

    def targets_of(turn):
        peer = jnp.where(turn < local_count, 0, me ^ (turn - local_count + 1))
        own = 2 * (turn - local_next)
        local_first = jnp.where(turn < local_next, turn, own)
        local_second = jnp.where(turn < local_next, turn + 1, own + 1)
        first = jnp.where(turn < local_count, local_first, pair_s[0, peer])
        second = jnp.where(turn < local_count, local_second, jnp.maximum(send_s[0, peer], 0))
        return first, second

    def stage_distance(turn, half):
        slot = slot_of(turn)
        first, second = targets_of(turn)
        data = in_msg[slot, 0:8, :]
        square = data * data
        total = pltpu.roll(square, 1, 0) + pltpu.roll(square, 2, 0) + pltpu.roll(square, 3, 0)
        p0, p1, p2 = three_pieces(jnp.where(weight_row, total, data))
        o0 = jnp.where(weight_row, 1.0, p0)
        o1 = jnp.where(weight_row, 1.0, p1)
        r0 = pltpu.roll(p0, 4, 0)
        r1 = pltpu.roll(p1, 4, 0)
        r2 = pltpu.roll(p2, 4, 0)
        s0 = pltpu.roll(o0, 4, 0)
        s1 = pltpu.roll(o1, 4, 0)
        far_len = in_msg[slot, 8:10, :]
        masses = jnp.where(row < 3, data[3:4, :], data[7:8, :])
        stack = jnp.concatenate(
            [
                jnp.where(upper, p0, s0),
                jnp.where(upper, o0, r1),
                jnp.where(upper, o1, r2),
                jnp.where(upper, r0, o0),
                jnp.where(upper, s0, p1),
                jnp.where(upper, s1, p2),
                jnp.where(row < 1, far_len[0:1, :], jnp.where(row < 2, far_len[1:2, :], masses)),
                jnp.zeros((8, slots), F32),
            ],
            axis=0,
        )
        turned = jnp.transpose(stack)
        right = jnp.concatenate([aug[first, 0], aug[second, 1]], axis=1)
        dist[half] = dot_plain(turned.astype(BF16), right)
        columns[half] = turned
        weight = jnp.where(upper, data[3:4, :], data[7:8, :])
        rows = weight * jnp.where(weight_row, 1.0, data)
        source_rows[slot] = rows
        m0, m1, m2 = three_pieces(rows)
        v0, v1, v2 = three_pieces(weight * total)
        v1 = pltpu.roll(v1, 7, 0)
        v2 = pltpu.roll(v2, 6, 0)
        squares = jnp.where(weight_row, v0, jnp.where((row == 2) | (row == 6), v1, v2))
        source_stack[half] = jnp.concatenate([m0, m1, m2, squares], axis=0).astype(BF16)

    def split_store(ref, index, block, lanes, value):
        top = value.astype(BF16)
        lanes = slice(lanes, lanes + slots)
        ref[index + (slice(block, block + CHUNK), lanes)] = top
        rest = (value - top.astype(F32)).astype(BF16)
        ref[index + (slice(slots + block, slots + block + CHUNK), lanes)] = rest

    def stage_terms(turn, half):
        slot = slot_of(turn)
        pair_targets = targets_of(turn)
        for side in range(2):
            len_i = table_len[pair_targets[side], 0:1, :]
            fourth = jnp.zeros((8, slots), F32)
            for block in range(0, slots, CHUNK):
                rows = slice(block, block + CHUNK)
                raw = jnp.maximum(dist[half, rows, side * slots : (side + 1) * slots], 1e-30)
                radius = raw * lax.rsqrt(raw)
                t_i = jnp.maximum(len_i - radius, 0.0)
                cube = t_i * t_i * t_i
                t_j = jnp.maximum(columns[half, rows, 48 + side : 49 + side] - radius, 0.0)
                split_store(near_mats, (half,), block, side * slots, cube)
                split_store(far_mats, (slot,), block, side * slots, t_j * t_j * t_j)
                term = cube * t_i * columns[half, rows, 50 + side : 51 + side]
                for at in range(0, CHUNK, 8):
                    fourth = fourth + term[at : at + 8, :]
            for shift in (4, 2, 1):
                fourth = fourth + pltpu.roll(fourth, shift, 0)
            fourths[half, side] = fourth

    def stacked_pieces(value):
        p0, p1, p2 = three_pieces(value)
        stack = jnp.concatenate([p0, p1, p2, jnp.zeros((8, slots), F32)], axis=0).astype(BF16)
        return jnp.concatenate([stack, stack], axis=1)

    def sum_pieces(value):
        return value[0:8, :] + value[8:16, :] + value[16:24, :]

    def target_rows(turn):
        first, second = targets_of(turn)
        return jnp.where(upper, table[first], table[second])

    def moments(first_sums, second_sums, turn):
        sums = jnp.where(upper, first_sums, second_sums)
        weight = jnp.where(upper, first_sums[3:4, :], second_sums[7:8, :])
        return target_rows(turn) * weight - sums

    def stage_sums(turn, half):
        slot = slot_of(turn)
        first, second = targets_of(turn)
        stack = source_stack[half]
        left = jnp.concatenate([stack, stack], axis=1)
        found = dot_plain(left, near_mats[half])

        def piece(at):
            return jnp.where(upper, found[at : at + 8, 0:slots], found[at : at + 8, slots:])

        cubes = piece(0) + piece(8) + piece(16)
        square = piece(24)
        fourth = jnp.where(upper, fourths[half, 0], fourths[half, 1])
        square = square + pltpu.roll(square, 1, 0) + pltpu.roll(square, 2, 0)
        place = jnp.where(upper, table[first], table[second])
        gap = jnp.where(upper, table_gap[first], table_gap[second])
        length = jnp.where(upper, table_len[first], table_len[second])
        weight = jnp.where(upper, cubes[3:4, :], cubes[7:8, :])
        cross = place * cubes
        cross = pltpu.roll(cross, 1, 0) + pltpu.roll(cross, 2, 0) + pltpu.roll(cross, 3, 0)
        dens = gap * weight + 2.0 * cross - square - 0.75 * length * fourth
        slope = place * weight - cubes
        results[pl.ds(slot, 8, stride=stride), :] = jnp.where(weight_row, dens, slope)

    def sums(turn, bank):
        stage_sums(2 * turn, 2 * bank)
        stage_sums(2 * turn + 1, 2 * bank + 1)

    def terms(turn, bank):
        stage_terms(2 * turn, 2 * bank)
        stage_terms(2 * turn + 1, 2 * bank + 1)

    def distances(turn, bank):
        stage_distance(2 * turn, 2 * bank)
        stage_distance(2 * turn + 1, 2 * bank + 1)

    def full_turn(turn, bank):
        for at in range(2):
            stage_terms(2 * turn + at, 2 * bank + at)
            stage_sums(2 * turn - 2 + at, 2 - 2 * bank + at)
            stage_distance(2 * turn + 2 + at, 2 - 2 * bank + at)

    turns = total_count // 2
    mixed = local_count // 2
    local_steps = (mixed - 2) // 2
    early_steps = 1

    def local_step(step, carry):
        full_turn(2 * step + 1, 1)
        full_turn(2 * step + 2, 0)
        return carry

    def far_step(step, carry):
        turn = 2 * step + mixed
        wait_in(step + 1, 4, in_msg, recv_sem)
        full_turn(turn, mixed % 2)
        full_turn(turn + 1, (mixed + 1) % 2)
        return carry

    distances(0, 0)
    terms(0, 0)
    distances(1, 1)
    lax.fori_loop(0, early_steps, local_step, 0)
    pl.semaphore_wait(ready_sem, ring - 1)

    def send(step, carry):
        copy_out(step, out_msg, in_msg, send_sem, recv_sem)
        return carry

    lax.fori_loop(1, peers, send, 0)
    lax.fori_loop(early_steps, local_steps, local_step, 0)
    for turn in range(2 * local_steps + 1, mixed):
        if turn == mixed - 1:
            wait_in(0, 1, in_msg, recv_sem)
        full_turn(turn, turn % 2)
    steps = (turns - 1 - mixed) // 2
    lax.fori_loop(0, steps, far_step, 0)
    rest = (peers - 2) % 4
    for turn in range(mixed + 2 * steps, turns - 1):
        wait_in(steps + 1, rest, in_msg, recv_sem)
        full_turn(turn, turn % 2)
    sums(turns - 2, turns % 2)
    terms(turns - 1, (turns - 1) % 2)
    sums(turns - 1, (turns - 1) % 2)

    spare = stride - peers
    cell_ids = lax.broadcasted_iota(jnp.int32, (cells, peers), 0)
    extra = lax.broadcasted_iota(jnp.int32, (cells, spare), 1)
    extra_cell = lax.broadcasted_iota(jnp.int32, (cells, spare), 0)
    own_turn = 2 * (extra - local_next)
    is_next = extra < local_next
    is_own = (extra >= local_next) & (extra < local_count)
    extra_first = jnp.where(is_next, extra, jnp.where(is_own, own_turn, -1))
    extra_second = jnp.where(is_next, extra + 1, jnp.where(is_own, own_turn + 1, -1))

    from_peer = lax.broadcasted_iota(jnp.int32, (peers, peers), 0)
    at_step = lax.broadcasted_iota(jnp.int32, (peers, peers), 1)
    order = jnp.where(from_peer == at_step ^ me, 1.0, 0.0).astype(BF16)

    def by_step(keys):
        wide_keys = jnp.broadcast_to(keys.astype(F32), (16, peers)).astype(BF16)
        return dot_plain(wide_keys, order)[0:1, :].astype(jnp.int32)

    def owner(keys, extra_keys):
        near = jnp.where(cell_ids == keys, 1.0, 0.0)
        local = jnp.where(extra_cell == extra_keys, 1.0, 0.0)
        return jnp.concatenate([near, local], axis=1).astype(BF16)

    owner_first = owner(by_step(pair_ref[...]), extra_first)
    owner_second = owner(by_step(send_ref[...]), extra_second)

    owners = jnp.concatenate([owner_first, owner_first, owner_second, owner_second], axis=1)

    def summed(quantity):
        parts = []
        for at in (quantity, quantity + 4):
            value = results[at * stride : (at + 1) * stride, :]
            top = value.astype(BF16)
            parts += [top, (value - top.astype(F32)).astype(BF16)]
        return dot_plain(owners, jnp.concatenate(parts, axis=0))

    lens = smooth_ref[...]
    len2 = lens * lens
    len4 = len2 * len2
    norm = KERNEL_NORM / (len4 * len4)
    cell_row = lax.broadcasted_iota(jnp.int32, (cells, slots), 0)
    limit = jnp.zeros((cells, slots), jnp.int32)
    for cell in range(cells):
        limit = jnp.where(cell_row == cell, counts_s[cell], limit)
    occupied = lax.broadcasted_iota(jnp.int32, (cells, slots), 1) < limit
    total = summed(3) * (4.0 * norm)
    safe = jnp.where(occupied, total, 1.0)
    pressure = entropy_ref[...] * jnp.exp(jnp.log(safe) * (-1.0 / 3.0))
    strength = jnp.where(occupied, pressure * (20.0 * norm), 0.0)
    out_ref[0] = jnp.where(occupied, total, 0.0)
    for cell in range(cells):
        table_press[cell] = jnp.broadcast_to(strength[cell : cell + 1, :], (8, slots))

    def send_press(step, carry):
        peer = me ^ step
        chosen = send_s[0, peer]
        first = jnp.where(chosen < 0, cells, chosen)
        second = pair_s[0, peer]
        out_press[step] = jnp.where(row < 1, table_press[first], table_press[second])[0:2, :]
        copy_out(step, out_press, in_press, send_sem2, recv_sem2)
        return carry

    lax.fori_loop(1, peers, send_press, 0, unroll=2)
    near_part = [summed(axis) * strength for axis in range(3)]

    def fill_press(index, first, second):
        in_press[peers + index, 0:1, :] = table_press[first, 0:1, :]
        in_press[peers + index, 1:2, :] = table_press[second, 0:1, :]

    for cell in range(local_next):
        fill_press(cell, cell + 1, cell)
    for turn in range(local_own):
        fill_press(local_next + turn, 2 * turn, 2 * turn + 1)

    def stage_force(turn):
        slot = slot_of(turn)
        press = jnp.where(upper, in_press[slot, 0:1, :], in_press[slot, 1:2, :])
        found = sum_pieces(dot_plain(stacked_pieces(source_rows[slot] * press), far_mats[slot]))
        slope = moments(found[:, 0:slots], found[:, slots : 2 * slots], turn)
        results[pl.ds(slot, 8, stride=stride), :] = slope

    for turn in range(local_count):
        stage_force(turn)

    def far_force(step, carry):
        for half in range(2):
            wait_in(2 * step + 1 + half, 4, in_press, recv_sem2)
        for at in range(8):
            stage_force(local_count + 1 + 8 * step + at)
        return carry

    wait_in(0, 1, in_press, recv_sem2)
    stage_force(local_count)
    steps = (peers - 2) // 8
    lax.fori_loop(0, steps, far_force, 0)
    tail = local_count + 1 + 8 * steps
    for at in range(tail, total_count, 4):
        wait_in((at - local_count + 3) // 4, min(4, total_count - at), in_press, recv_sem2)
    for at in range(tail, total_count):
        stage_force(at)
    for axis in range(3):
        out_ref[1 + axis] = jnp.where(occupied, near_part[axis] + summed(axis), 0.0)

    def drain(ref, sem):
        moved = ref.at[pl.ds(0, peers - 1)]
        pltpu.make_async_copy(moved, moved, sem).wait()

    drain(out_msg, send_sem)
    drain(out_press, send_sem2)


def split_kernel(found_ref, density_ref, accel_ref):
    density_ref[...] = found_ref[0]
    accel_ref[...] = found_ref[1:4]


def on_device(send_cells, pair_cell, counts, positions, mass, smooth, entropy):
    cells, slots = mass.shape
    peers = lax.axis_size(("cells", "sub"))
    ring = lax.axis_size("sub")
    chosen = send_cells.reshape(1, peers)
    partner = pair_cell.reshape(1, peers)
    stride = peers + 32
    vmem = pl.BlockSpec(memory_space=pltpu.VMEM)
    smem = pl.BlockSpec(memory_space=pltpu.SMEM)
    found = pl.pallas_call(
        functools.partial(pair_kernel, ring, peers, cells, slots),
        out_shape=jax.ShapeDtypeStruct((4, cells, slots), F32),
        in_specs=[smem, smem, smem] + [vmem] * 6,
        out_specs=vmem,
        scratch_shapes=[
            pltpu.VMEM((cells + 1, 8, slots), F32),
            pltpu.VMEM((cells + 1, 8, slots), F32),
            pltpu.VMEM((cells + 1, 8, slots), F32),
            pltpu.VMEM((cells, 8, slots), F32),
            pltpu.VMEM((4, slots, 64), F32),
            pltpu.VMEM((4, 2, 8, slots), F32),
            pltpu.VMEM((cells, 2, 64, slots), BF16),
            pltpu.VMEM((peers, 10, slots), F32),
            pltpu.VMEM((stride, 10, slots), F32),
            pltpu.VMEM((peers, 2, slots), F32),
            pltpu.VMEM((stride, 2, slots), F32),
            pltpu.VMEM((stride, 8, slots), F32),
            pltpu.VMEM((4, 32, slots), BF16),
            pltpu.VMEM((4, slots, 2 * slots), F32),
            pltpu.VMEM((4, 2 * slots, 2 * slots), BF16),
            pltpu.VMEM((stride, 2 * slots, 2 * slots), BF16),
            pltpu.VMEM((8 * stride, slots), F32),
            pltpu.SemaphoreType.DMA,
            pltpu.SemaphoreType.DMA(((peers + 1) // 4 + 1,)),
            pltpu.SemaphoreType.DMA,
            pltpu.SemaphoreType.DMA(((peers + 1) // 4 + 1,)),
            pltpu.SemaphoreType.REGULAR,
        ],
        compiler_params=pltpu.CompilerParams(
            collective_id=0, has_side_effects=True, vmem_limit_bytes=56 * 2**20
        ),
        name="cell_pairs",
    )(chosen, partner, counts, chosen, partner, positions, mass, smooth, entropy)
    return pl.pallas_call(
        split_kernel,
        out_shape=(
            jax.ShapeDtypeStruct((cells, slots), F32),
            jax.ShapeDtypeStruct((3, cells, slots), F32),
        ),
        in_specs=[vmem],
        out_specs=(vmem, vmem),
        name="split_outputs",
    )(found)


def solution(mesh):
    in_specs = (
        P(("cells", "sub"), None, None),
        P(("cells", "sub"), None, None),
        P(("cells", "sub")),
        P(None, ("cells", "sub"), None),
        P(("cells", "sub"), None),
        P(("cells", "sub"), None),
        P(("cells", "sub"), None),
    )
    out_specs = (P(("cells", "sub"), None), P(None, ("cells", "sub"), None))
    return jax.shard_map(
        on_device, mesh=mesh, in_specs=in_specs, out_specs=out_specs, check_vma=False
    )
```

profile of v0, /device:TPU:1, one launch (start us, length us, event | category | flops | bytes accessed | tf_op | source)
XLA Modules:
  0.0 47.0 jit_solution(6100296418418638727)
XLA Ops:
  0.6 45.0 %cell_pairs.1.found_ref = f32[4,16,128]{2,1,0:T(8,128)} custom-call(s32[1,128]{1,0:T(1,128)} %bitcast.2, s32[1,128]{1,0:T(1,128)} %bitcast.4, s32[16]{0:T(128)} %counts_s.1, s32[1,128]{1,0:T(1,128)} %bitcast.3, s32[1,128]{1,0:T(1,128)} %bitcast.5, f32[3,16,128]{2,1,0:T(8,128)} %pos_ref.1, f32[16,128]{1,0:T(8,128)} %mass_ref.1, f32[16,128]{1,0:T(8,128)} %smooth_ref.1, ...), custom_call_target="tpu_custom_call" | custom-call | tf_op jit(solution)/shard_map/cell_pairs/pallas_call | solution.py:477
  45.6 1.4 %split_outputs.1 = (f32[16,128]{1,0:T(8,128)}, f32[3,16,128]{2,1,0:T(8,128)}) custom-call(f32[4,16,128]{2,1,0:T(8,128)} %cell_pairs.1.found_ref), custom_call_target="tpu_custom_call" | custom-call | tf_op jit(solution)/shard_map/split_outputs/pallas_call | solution.py:511
where the time goes:
time: 47.2 us; the launch traced here: 47 us
  Pallas kernels  46.3 us (98%)
  between operations  0.64 us (1%)
    pallas_call x1, Pallas kernels, on_device(): pl.pallas_call(functools.partial(pair_kernel, ring, peers, cells, slots),...  45 us
    pallas_call x1, Pallas kernels, on_device(): pl.pallas_call(split_kernel, out_shape=(jax.ShapeDtypeStruct((cells, slot...  1.37 us

commit v1 on v0

--- a/solution.py
+++ b/solution.py
@@ -434,17 +434,17 @@
         stage_force(turn)
 
     def far_force(step, carry):
-        for half in range(2):
-            wait_in(2 * step + 1 + half, 4, in_press, recv_sem2)
-        for at in range(8):
-            stage_force(local_count + 1 + 8 * step + at)
+        for half in range(4):
+            wait_in(4 * step + 1 + half, 4, in_press, recv_sem2)
+        for at in range(16):
+            stage_force(local_count + 1 + 16 * step + at)
         return carry
 
     wait_in(0, 1, in_press, recv_sem2)
     stage_force(local_count)
-    steps = (peers - 2) // 8
+    steps = (peers - 2) // 16
     lax.fori_loop(0, steps, far_force, 0)
-    tail = local_count + 1 + 8 * steps
+    tail = local_count + 1 + 16 * steps
     for at in range(tail, total_count, 4):
         wait_in((at - local_count + 3) // 4, min(4, total_count - at), in_press, recv_sem2)
     for at in range(tail, total_count):

time: 47.2 us -> 46.4 us (0.983)
  Pallas kernels: 46.3 us -> 45.5 us
    pallas_call x1, Pallas kernels: 45 us -> 44.1 us  [on_device(): pl.pallas_call(functools.partial(pair_kernel, ring, peers, cells, slots),...]
where the time goes in v1:
time: 46.4 us; the launch traced here: 46.2 us
  Pallas kernels  45.5 us (98%)
  between operations  0.64 us (1%)
    pallas_call x1, Pallas kernels, on_device(): pl.pallas_call(functools.partial(pair_kernel, ring, peers, cells, slots),...  44.1 us
    pallas_call x1, Pallas kernels, on_device(): pl.pallas_call(split_kernel, out_shape=(jax.ShapeDtypeStruct((cells, slot...  1.37 us

profile of v1, /device:TPU:1, one launch (start us, length us, event | category | flops | bytes accessed | tf_op | source)
XLA Modules:
  0.0 46.2 jit_solution(4474337412941664239)
XLA Ops:
  0.6 44.1 %cell_pairs.1.found_ref = f32[4,16,128]{2,1,0:T(8,128)} custom-call(s32[1,128]{1,0:T(1,128)} %bitcast.2, s32[1,128]{1,0:T(1,128)} %bitcast.4, s32[16]{0:T(128)} %counts_s.1, s32[1,128]{1,0:T(1,128)} %bitcast.3, s32[1,128]{1,0:T(1,128)} %bitcast.5, f32[3,16,128]{2,1,0:T(8,128)} %pos_ref.1, f32[16,128]{1,0:T(8,128)} %mass_ref.1, f32[16,128]{1,0:T(8,128)} %smooth_ref.1, ...), custom_call_target="tpu_custom_call" | custom-call | tf_op jit(solution)/shard_map/cell_pairs/pallas_call | solution.py:477
  44.8 1.4 %split_outputs.1 = (f32[16,128]{1,0:T(8,128)}, f32[3,16,128]{2,1,0:T(8,128)}) custom-call(f32[4,16,128]{2,1,0:T(8,128)} %cell_pairs.1.found_ref), custom_call_target="tpu_custom_call" | custom-call | tf_op jit(solution)/shard_map/split_outputs/pallas_call | solution.py:511
